TPU v7x, 256 devices: a whole 4x4x8 slice. The times are simulated.
256 devices in a mesh: row: 8 (over y, x_lo), col: 32 (over z, x_hi, core).
Axes of the slice: x: 4 (x_hi: 2, x_lo: 2; x = x_hi * 2 + x_lo), y: 4, z: 8, core: 2. Of those that a mesh axis runs over, the one named last changes fastest.
Arguments:
- source_embed: bfloat16 [64, 49152], P(None, ('row', 'col')), may hold values from -0.8984375 to 0.8984375
- target_embed: bfloat16 [64, 49152], P(None, ('row', 'col')), may hold values from -0.8984375 to 0.8984375
- left_factor: bfloat16 [128, 49152], P(None, ('row', 'col')), may hold values from -6 to 6
- right_factor: bfloat16 [128, 49152], P(None, ('row', 'col')), may hold values from -0.01953125 to 0.01953125
Outputs:
- source_grad: float32 [64, 49152], P(None, ('row', 'col'))
- target_grad: float32 [64, 49152], P(None, ('row', 'col'))
All inputs are finite; a program needn't handle non-finite values.
Results may differ from a plain program's by a relative error of at most 0.0055.
Values may be sent and summed in bfloat16 or wider, within the bound.
A program may use at most 64 MiB of HBM per device.

v0:
```python
import math

import jax
import jax.numpy as jnp
from jax import lax
from jax.sharding import PartitionSpec as P

kernel_rate = 0.5


def weighted_tile(rows_embed, rows_factor, cols_embed, cols_factor, cols_square):
    rows_square = jnp.sum(jnp.square(rows_embed.astype(jnp.float32)), axis=0)
    cross = lax.dot_general(
        rows_embed, cols_embed, (((0,), (0,)), ((), ())), preferred_element_type=jnp.float32
    )
    distance = rows_square[:, None] + cols_square[None, :] - 2.0 * cross
    kernel = jnp.exp(-kernel_rate * distance)
    adjoint = lax.dot_general(
        rows_factor, cols_factor, (((0,), (0,)), ((), ())), preferred_element_type=jnp.float32
    )
    return (adjoint * kernel).astype(jnp.bfloat16)


def tile_terms(rows_embed, rows_factor, cols_embed, cols_factor, cols_square):
    weighted = weighted_tile(rows_embed, rows_factor, cols_embed, cols_factor, cols_square)
    weighted_wide = weighted.astype(jnp.float32)
    row_pull = lax.dot_general(
        cols_embed, weighted, (((1,), (1,)), ((), ())), preferred_element_type=jnp.float32
    )
    row_mass = jnp.sum(weighted_wide, axis=1)
    col_pull = jnp.dot(rows_embed, weighted, preferred_element_type=jnp.float32)
    col_mass = jnp.sum(weighted_wide, axis=0)
    return (row_pull, row_mass, col_pull, col_mass)


def sweep_rows(rows_all, factors_all, cols_embed, cols_factor, cols_square, totals, offset):
    length = rows_all.shape[1]
    block_rows = math.gcd(length, 1024)
    steps_count = length // block_rows

    def visit_block(counter, current):
        begin_at = counter * block_rows
        rows_embed = lax.dynamic_slice_in_dim(rows_all, begin_at, block_rows, 1)
        rows_factor = lax.dynamic_slice_in_dim(factors_all, begin_at, block_rows, 1)
        row_pull, row_mass, col_pull, col_mass = tile_terms(
            rows_embed, rows_factor, cols_embed, cols_factor, cols_square
        )
        place = offset + begin_at
        first = lax.dynamic_update_slice_in_dim(current[0], row_pull, place, 1)
        second = lax.dynamic_update_slice_in_dim(current[1], row_mass[None, :], place, 1)
        return (first, second, current[2] + col_pull, current[3] + col_mass[None, :])

    return lax.fori_loop(0, steps_count, visit_block, totals)


def finish_columns(col_pull, col_mass, target_embed):
    pulled_cols, massed_cols = (
        lax.psum_scatter(col_pull, "row", scatter_dimension=1, tiled=True),
        lax.psum_scatter(col_mass, "row", scatter_dimension=1, tiled=True),
    )
    return 2.0 * kernel_rate * (pulled_cols - massed_cols * target_embed.astype(jnp.float32))


def per_device(source_embed, target_embed, left_factor, right_factor):
    cols_embed, cols_factor = (
        lax.all_gather(target_embed, "row", axis=1, tiled=True),
        lax.all_gather(right_factor, "row", axis=1, tiled=True),
    )
    cols_square = jnp.sum(jnp.square(cols_embed.astype(jnp.float32)), axis=0)
    embed_width = source_embed.shape[0]
    own_rows = source_embed.shape[1]
    rows_total = own_rows * lax.axis_size("col")
    cols_total = cols_embed.shape[1]
    own_embed = source_embed.astype(jnp.float32)
    col_start = (
        jnp.zeros((embed_width, cols_total), jnp.float32),
        jnp.zeros((1, cols_total), jnp.float32),
    )
    totals = (
        jnp.zeros((embed_width, rows_total), jnp.float32),
        jnp.zeros((1, rows_total), jnp.float32),
    ) + col_start
    rows_embed, rows_factor = (
        lax.all_gather(source_embed, "col", axis=1, tiled=True),
        lax.all_gather(left_factor, "col", axis=1, tiled=True),
    )
    totals = sweep_rows(rows_embed, rows_factor, cols_embed, cols_factor, cols_square, totals, 0)
    pulled, massed = (
        lax.psum_scatter(totals[0], "col", scatter_dimension=1, tiled=True),
        lax.psum_scatter(totals[1], "col", scatter_dimension=1, tiled=True),
    )
    source_grad = -2.0 * kernel_rate * (massed * own_embed - pulled)
    col_pull_part = totals[-2]
    col_mass_part = totals[-1]
    target_grad = finish_columns(col_pull_part, col_mass_part, target_embed)
    return (source_grad, target_grad)


def solution(mesh):
    in_specs = (
        P(None, ("row", "col")),
        P(None, ("row", "col")),
        P(None, ("row", "col")),
        P(None, ("row", "col")),
    )
    out_specs = (P(None, ("row", "col")), P(None, ("row", "col")))
    return jax.shard_map(
        per_device, mesh=mesh, in_specs=in_specs, out_specs=out_specs, check_vma=False
    )
```

profile of v0, /device:TPU:1, one launch (start us, length us, event | category | flops | bytes accessed | tf_op | source)
XLA Modules:
  0.0 523.4 jit_solution(9742843131764461443)
XLA Ops:
  7.2 0.0 all-gather.4.cloned.1.call-start
  7.2 0.7 all-gather.4.cloned.1.call-update
  7.9 0.0 reduce-scatter.19.cloned.1.call-start
  8.0 25.1 %all-gather.1 = bf16[8,192,64]{1,2,0:T(8,128)(2,1)S(1)} all-gather(bf16[1,192,64]{1,2,0:T(8,128)(2,1)} %bitcast.52), channel_id=1, replica_groups=mesh['row'=8,'col'=32] {'row'}, dimensions={0}, use_global_device_ids=true | all-gather | bytes 221184 | tf_op jit(solution)/shard_map/all_gather | solution.py:66
  33.1 0.1 copy.13
  33.3 0.2 reshape.9
  33.5 53.5 %all-gather = bf16[32,192,64]{1,2,0:T(8,128)(2,1)S(1)} all-gather(bf16[1,192,64]{1,2,0:T(8,128)(2,1)} %bitcast.53), channel_id=1, replica_groups=mesh['row'=8,'col'=32] {'col'}, dimensions={0}, use_global_device_ids=true | all-gather | bytes 811008 | tf_op jit(solution)/shard_map/all_gather | solution.py:84
  87.0 0.6 copy.12
  87.6 2.0 reshape.7
  89.6 23.4 %all_gather.13 = bf16[128,1536]{0,1:T(8,128)(2,1)S(1)} all-gather(bf16[128,192]{0,1:T(8,128)(2,1)S(1)} %copy-done.4), channel_id=1, replica_groups=mesh['row'=8,'col'=32] {'row'}, dimensions={1}, use_global_device_ids=true | all-gather | bytes 442368 | tf_op jit(solution)/shard_map/all_gather | solution.py:67
  113.0 0.9 copy.15
  113.9 0.1 multiply_reduce_fusion.1
  113.9 0.0 all-gather.4.cloned.1.call-done
  114.0 1.3 broadcast_in_dim.32
  115.3 64.3 %while.20 = (s32[]{:T(128)}, f32[64,6144]{1,0:T(8,128)}, f32[1,6144]{1,0:T(1,128)S(1)}, f32[64,1536]{1,0:T(8,128)}, f32[1,1536]{1,0:T(1,128)S(1)}, /*index=5*/bf...) while((s32[]{:T(128)}, f32[64,6144]{1,0:T(8,128)}, ...), condition=%wide.region_5.0_spmd.clone, body=%wide.region_1.0_spmd.clone.sunk | while | flops 1021181440 | bytes 26134768 | solution.py:53
  115.3 2.0 fusion.31
  117.2 0.9 multiply_reduce_fusion.3
  118.2 3.5 convert_reduce_fusion.3
  121.7 1.8 fusion.32
  123.5 2.3 convolution_add_fusion.2
  125.9 2.0 fusion.31
  127.8 0.9 multiply_reduce_fusion.3
  128.8 3.5 convert_reduce_fusion.3
  132.3 1.8 fusion.32
  134.1 2.5 convolution_add_fusion.2
  136.6 2.0 fusion.31
  138.6 0.9 multiply_reduce_fusion.3
  139.5 3.5 convert_reduce_fusion.3
  143.0 1.8 fusion.32
  144.8 2.5 convolution_add_fusion.2
  147.3 2.0 fusion.31
  149.3 0.9 multiply_reduce_fusion.3
  150.3 3.5 convert_reduce_fusion.3
  153.8 1.8 fusion.32
  155.6 2.5 convolution_add_fusion.2
  158.1 2.0 fusion.31
  160.1 0.9 multiply_reduce_fusion.3
  161.0 3.5 convert_reduce_fusion.3
  164.5 1.8 fusion.32
  166.3 2.5 convolution_add_fusion.2
  168.8 2.0 fusion.31
  170.8 0.9 multiply_reduce_fusion.3
  171.8 3.5 convert_reduce_fusion.3
  175.3 1.8 fusion.32
  177.1 2.5 convolution_add_fusion.2
  179.6 1.2 copy.22
  180.8 0.0 reduce-scatter.19.cloned.1.call-update
  180.9 0.0 reduce-scatter.13.cloned.1.call-start
  180.9 2.2 copy.16
  183.1 0.0 reduce-scatter.13.cloned.1.call-update
  183.1 0.0 reduce-scatter.17.cloned.1.call-start
  183.2 1.2 copy.20
  184.5 0.0 reduce-scatter.15.cloned.1.call-start
  184.5 3.3 copy.18
  187.9 31.4 %reduce-scatter.19.cloned.1.call-done = f32[192,1]{1,0:T(8,128)} async-done(((f32[1536,1]{1,0:T(8,128)}), f32[192,1]{1,0:T(8,128)}) %reduce-scatter.19.cloned.1.call-update) | async-done | bytes 784
  219.3 1.0 copy.23
  220.3 125.7 %reduce-scatter.13.cloned.1.call-done = f32[192,1]{1,0:T(8,128)} async-done(((f32[6144,1]{1,0:T(8,128)}), f32[192,1]{1,0:T(8,128)}) %reduce-scatter.13.cloned.1.call-update) | async-done | bytes 784
  346.0 1.0 copy.17
  346.9 41.8 %reduce-scatter.17.cloned.1.call-done = f32[192,64]{1,0:T(8,128)} async-done(((f32[1536,64]{1,0:T(8,128)}), f32[192,64]{1,0:T(8,128)}) %reduce-scatter.17.cloned.1.call-update) | async-done | bytes 49168
  388.7 1.0 copy.21
  389.7 0.6 multiply_subtract_fusion
  390.4 124.9 %reduce-scatter.15.cloned.1.call-done = f32[192,64]{1,0:T(8,128)} async-done(((f32[6144,64]{1,0:T(8,128)}), f32[192,64]{1,0:T(8,128)}) %reduce-scatter.15.cloned.1.call-update) | async-done | bytes 49168
  515.2 1.0 copy.19
  516.2 0.6 subtract_multiply_fusion
  (37 shorter events, 0.2 us)
Async XLA Ops:
  7.2 106.8 %all-gather.4.cloned.1.call-start = ((), (), s32[]{:S(2)}) async-start(), calls=%async_computation.4 | async-start | bytes 1622016 | tf_op jit(solution)/shard_map/all_gather | solution.py:85
  7.9 211.4 %reduce-scatter.19.cloned.1.call-start = ((), (), s32[]{:S(2)}) async-start(), calls=%async_computation.8 | async-start | bytes 884736
  8.0 81.6 %copy-start.4 = (bf16[128,192]{0,1:T(8,128)(2,1)S(1)}, bf16[128,192]{0,1:T(8,128)(2,1)}, u32[]{:S(2)}) copy-start(bf16[128,192]{0,1:T(8,128)(2,1)} %param.9) | copy-start | bytes 147460
  115.3 2.9 copy-start.1
  125.9 2.9 copy-start.1
  136.6 2.9 copy-start.1
  147.3 2.9 copy-start.1
  158.1 2.9 copy-start.1
  168.8 2.9 copy-start.1
  180.9 165.1 %reduce-scatter.13.cloned.1.call-start = ((), (), s32[]{:S(2)}) async-start(), calls=%async_computation.5 | async-start | bytes 3244032
  180.9 2.3 copy-start
  183.1 205.6 %reduce-scatter.17.cloned.1.call-start = ((), (), s32[]{:S(2)}) async-start(), calls=%async_computation.7 | async-start | bytes 884736
  184.5 330.8 %reduce-scatter.15.cloned.1.call-start = ((), (), s32[]{:S(2)}) async-start(), calls=%async_computation.6 | async-start | bytes 3244032
  184.5 205.2 %copy-start.2 = (bf16[64,192]{1,0:T(8,128)(2,1)S(1)}, bf16[64,192]{1,0:T(8,128)(2,1)}, u32[]{:S(2)}) copy-start(bf16[64,192]{1,0:T(8,128)(2,1)} %param.7) | copy-start | bytes 73732
  184.5 331.7 %copy-start.3 = (bf16[64,192]{1,0:T(8,128)(2,1)S(1)}, bf16[64,192]{1,0:T(8,128)(2,1)}, u32[]{:S(2)}) copy-start(bf16[64,192]{1,0:T(8,128)(2,1)} %param.6) | copy-start | bytes 73732
Sparse Core Ops, SparseCore 0:
  10.8 83.7 all-gather.3
  181.0 38.2 reduce-scatter.18
  224.1 121.8 reduce-scatter.12
  348.4 40.3 reduce-scatter.16
  393.3 121.8 reduce-scatter.14
where the time goes:
time: 528 us; the launch traced here: 523 us
  waiting for transfers between devices  325 us (62%)
  blocking collectives  102 us (19%)
  matrix products  58.2 us (11%)
  local copies, waits for them, and re-layouts  17.2 us (3%)
  between operations  13.9 us (3%)
  other arithmetic  7.14 us (1%)
    unnamed x9, waiting for transfers between devices  325 us
    all_gather x1, blocking collectives, per_device(): lax.all_gather(source_embed, 'col', axis=1, tiled=True)  53.5 us
    all_gather x1, blocking collectives, per_device(): lax.all_gather(target_embed, 'row', axis=1, tiled=True)  25.1 us
    all_gather x1, blocking collectives, per_device(): lax.all_gather(right_factor, 'row', axis=1, tiled=True)  23.4 us
    dot_general x6, matrix products, weighted_tile(): lax.dot_general(rows_factor, cols_factor, (((0,), (0,)), ((), ())), prefe...  21 us
    unnamed x19, local copies, waits for them, and re-layouts  15.1 us
    dot_general x6, matrix products, tile_terms(): col_pull = jnp.dot(rows_embed, weighted, preferred_element_type=jnp.float32)  14.8 us
    dot_general x6, matrix products, weighted_tile(): lax.dot_general(rows_embed, cols_embed, (((0,), (0,)), ((), ())), preferr...  11.7 us
  transfers between devices with their start and end apart: 5, of which 4 were waited for; matrix products, arithmetic and copies ran while one was open for 3% of the time, Pallas kernels for 0%

commit v1 on v0

v1 whole, which is shorter than its diff:
```python
import functools

import jax
import jax.numpy as jnp
from jax import lax
from jax.experimental import pallas as pl
from jax.experimental.pallas import tpu as pltpu
from jax.sharding import PartitionSpec as P

MESH = pl.DeviceIdType.MESH
f32, bf16 = jnp.float32, jnp.bfloat16

E = 64
R = 128
B = 192
LANES = E + 64 + R
GROUP = 16
CHUNK = 4 * B
ONE_X, ONE_Y = E + 3, E

PLANE = [(0, 0), (1, 0), (3, 0), (0, 1), (0, 3), (1, 1), (3, 3), (1, 3), (3, 1), (2, 0), (0, 2), (2, 1), (2, 3), (1, 2), (3, 2), (2, 2)]
LINE = [(0, 0), (0, 1), (1, 0), (7, 0), (1, 1), (7, 1), (2, 0), (6, 0), (2, 1), (6, 1), (3, 0), (5, 0), (3, 1), (5, 1), (4, 0), (4, 1)]

ORDER = [(0, 0), (0, 1), (1, 0), (1, 1), (0, 2), (1, 2), (2, 0), (2, 1), (2, 2), (0, 3), (1, 3), (2, 3), (3, 0), (3, 1), (3, 2), (3, 3)]

NN = (((1,), (0,)), ((), ()))
NT = (((1,), (1,)), ((), ()))


def dot(a, b, dims):
    return lax.dot_general(a, b, dims, preferred_element_type=f32)


def prepare(embed_ref, factor_ref, first, rows_ref, stack):
    wide = embed_ref[...].astype(f32)
    half = -0.5 * jnp.sum(wide * wide, axis=0, keepdims=True)
    high = half.astype(bf16).astype(f32)
    middle = (half - high).astype(bf16).astype(f32)
    low = half - high - middle
    place = lax.broadcasted_iota(jnp.int32, (E, B), 0)
    norms, ones = (0, 3) if first else (3, 0)
    extra = jnp.where((place >= ones) & (place < ones + 3), 1.0, 0.0)
    for at, piece in enumerate((high, middle, low)):
        extra = jnp.where(place == norms + at, piece, extra)
    stack[0:E, :] = embed_ref[...]
    stack[E : 2 * E, :] = extra.astype(bf16)
    stack[2 * E : LANES, :] = factor_ref[...]
    down = lax.broadcasted_iota(jnp.int32, (B, B), 0)
    along = lax.broadcasted_iota(jnp.int32, (B, B), 1)
    unit = jnp.where(down == along, 1.0, 0.0).astype(bf16)
    rows_ref[0:B, :] = dot(unit, stack[...], NT).astype(bf16)


def pack(block):
    lane = lax.broadcasted_iota(jnp.int32, (B // 2, 128), 1)
    return jnp.where(lane < E, block[0 : B // 2], pltpu.roll(block[B // 2 :], E, 1)).astype(bf16)


def unpack(total, out_ref):
    tall = jnp.concatenate([total, jnp.zeros((128 - B // 2, 128), f32)], axis=0).T
    lane = lax.broadcasted_iota(jnp.int32, (E, 128), 1)
    later = pltpu.roll(tall[E:, :], B // 2, 1)
    out_ref[:, 0:128] = jnp.where(lane < B // 2, tall[0:E, :], later)
    out_ref[:, 128:B] = later[:, 0 : B - 128]


def kernel(source, target, left, right, out_s, out_t, xa, ya, xt, rp, cp, stack, send_r, send_c, recv_r, recv_c, *sems):
    gx_s, gx_r, gy_s, gy_r, rr_s, rr_r, rc_s, rc_r = sems
    row, col = lax.axis_index("row"), lax.axis_index("col")
    y, z, core = row // 2, col // 4, col % 2
    x = (col // 2) % 2 * 2 + row % 2

    def device(x, y, z, core):
        return (y * 2 + x % 2, (z * 2 + x // 2) * 2 + core)

    plane = [device((x + dx) % 4, (y + dy) % 4, z, core) for dx, dy in PLANE]
    line = [device(x, y, (z + dz) % 8, (core + dc) % 2) for dz, dc in LINE]
    plane_owner = [device((x + 4 - dx) % 4, (y + 4 - dy) % 4, z, core) for dx, dy in PLANE]
    line_owner = [device(x, y, (z + 8 - dz) % 8, (core + 2 - dc) % 2) for dz, dc in LINE]

    def copy(src, dst, send, recv, peer):
        return pltpu.make_async_remote_copy(
            src_ref=src, dst_ref=dst, send_sem=send, recv_sem=recv, device_id=peer, device_id_type=MESH
        )

    def gather_x(k):
        return copy(xa.at[pl.ds(0, B), :], xa.at[pl.ds(k * B, B), :], gx_s.at[k], gx_r.at[k], plane[k])

    def gather_y(k):
        return copy(ya.at[pl.ds(0, B), :], ya.at[pl.ds(k * B, B), :], gy_s.at[k], gy_r.at[k], line[k])

    def give_r(k):
        return copy(send_r.at[k], recv_r.at[k], rr_s.at[k], rr_r.at[k], plane_owner[k])

    def give_c(k):
        return copy(send_c.at[k], recv_c.at[k], rc_s.at[k], rc_r.at[k], line_owner[k])

    barrier = pltpu.get_barrier_semaphore()
    for k in range(1, GROUP):
        pl.semaphore_signal(barrier, inc=1, device_id=plane[k], device_id_type=MESH)
        pl.semaphore_signal(barrier, inc=1, device_id=line[k], device_id_type=MESH)
    prepare(source, left, True, xa, stack)
    prepare(target, right, False, ya, stack)
    pl.semaphore_wait(barrier, 2 * (GROUP - 1))
    for k in range(1, GROUP):
        gather_x(k).start()
        gather_y(k).start()
    rp[...] = jnp.zeros_like(rp)
    cp[...] = jnp.zeros_like(cp)

    def arrive_x(chunk):
        for k in range(max(4 * chunk, 1), 4 * chunk + 4):
            gather_x(k).wait_recv()
        rows = slice(chunk * CHUNK, (chunk + 1) * CHUNK)
        xt[:, rows] = xa[rows, 0:128].T

    def arrive_y(chunk):
        for k in range(max(4 * chunk, 1), 4 * chunk + 4):
            gather_y(k).wait_recv()

    def finish(pulls, mass, embeds, chunk, send, recv, give):
        grads = pulls - pulls[:, mass : mass + 1] * embeds.astype(f32)
        for i in range(4):
            k = 4 * chunk + i
            packed = pack(grads[i * B : (i + 1) * B])
            if k == 0:
                recv[0] = packed
            else:
                send[k] = packed
                give(k).start()

    def tile(t, _):
        rb = sum(jnp.where(t == i, r, 0) for i, (r, _) in enumerate(ORDER))
        cb = sum(jnp.where(t == i, c, 0) for i, (_, c) in enumerate(ORDER))
        for i, (r, c) in enumerate(ORDER):
            new_x = all(r != a for a, _ in ORDER[:i])
            new_y = all(c != a for _, a in ORDER[:i])
            if new_x or new_y:

                @pl.when(t == i)
                def _():
                    if new_x:
                        arrive_x(r)
                    if new_y:
                        arrive_y(c)

        rows = pl.ds(pl.multiple_of(rb * CHUNK, CHUNK), CHUNK)
        cols = pl.ds(pl.multiple_of(cb * CHUNK, CHUNK), CHUNK)
        arg = dot(xa[rows, 0:128], ya[cols, 0:128], NT)
        adjoint = dot(xa[rows, 128:256], ya[cols, 128:256], NT)
        weighted = (adjoint * jnp.exp(arg)).astype(bf16)
        rp[rows, :] += dot(weighted, ya[cols, 0:128], NN)
        cp[0:80, cols] += dot(xt[0:80, rows], weighted, NN)

        for i, (r, c) in enumerate(ORDER):
            last_x = all(r != a for a, _ in ORDER[i + 1 :])
            last_y = all(c != a for _, a in ORDER[i + 1 :])
            if last_x or last_y:

                @pl.when(t == i)
                def _():
                    if last_x:
                        at = slice(r * CHUNK, (r + 1) * CHUNK)
                        finish(rp[at, :], ONE_Y, xa[at, 0:128], r, send_r, recv_r, give_r)
                    if last_y:
                        at = slice(c * CHUNK, (c + 1) * CHUNK)
                        finish(cp[:, at].T, ONE_X, ya[at, 0:128], c, send_c, recv_c, give_c)

        return 0

    lax.fori_loop(0, len(ORDER), tile, 0)

    for recv, give, out in ((recv_r, give_r, out_s), (recv_c, give_c, out_t)):
        total = recv[0].astype(f32)
        for k in range(1, GROUP):
            give(k).wait_recv()
            total = total + recv[k].astype(f32)
        unpack(total, out)
    for k in range(1, GROUP):
        for each in (gather_x, gather_y, give_r, give_c):
            each(k).wait_send()


def per_device(source_embed, target_embed, left_factor, right_factor):
    frames = GROUP * B
    vmem = pl.BlockSpec(memory_space=pltpu.VMEM)
    return pl.pallas_call(
        kernel,
        out_shape=(jax.ShapeDtypeStruct((E, B), f32),) * 2,
        in_specs=[vmem] * 4,
        out_specs=(vmem,) * 2,
        scratch_shapes=[
            pltpu.VMEM((frames, LANES), bf16),
            pltpu.VMEM((frames, LANES), bf16),
            pltpu.VMEM((128, frames), bf16),
            pltpu.VMEM((frames, 128), f32),
            pltpu.VMEM((128, frames), f32),
            pltpu.VMEM((LANES, B), bf16),
        ]
        + [pltpu.VMEM((GROUP, B // 2, 128), bf16)] * 4
        + [pltpu.SemaphoreType.DMA((GROUP,))] * 8,
        compiler_params=pltpu.CompilerParams(
            collective_id=0, has_side_effects=True, vmem_limit_bytes=48 << 20
        ),
        cost_estimate=pl.CostEstimate(
            flops=2 * frames * frames * (2 * E + 2 * E + R), bytes_accessed=1 << 18, transcendentals=frames * frames
        ),
    )(source_embed, target_embed, left_factor, right_factor)


def solution(mesh):
    spec = P(None, ("row", "col"))
    return jax.shard_map(
        per_device, mesh=mesh, in_specs=(spec,) * 4, out_specs=(spec,) * 2, check_vma=False
    )
```

time: 528 us -> 69.6 us (0.13)
  the two profiles are of different devices: /device:TPU:1 before, /device:TPU:37 now
where the time goes in v1:
time: 69.6 us; the launch traced here: 69.4 us
  Pallas kernels  65.8 us (95%)
  local copies, waits for them, and re-layouts  2.93 us (4%)
    pallas_call x1, Pallas kernels, per_device(): pl.pallas_call(kernel, out_shape=(jax.ShapeDtypeStruct((E, B), f32),) * 2...  65.8 us
    unnamed x10, local copies, waits for them, and re-layouts  2.93 us

profile of v1, /device:TPU:37, one launch (start us, length us, event | category | flops | bytes accessed | tf_op | source)
XLA Modules:
  0.0 69.4 jit_solution(2222701513157293762)
XLA Ops:
  0.6 0.0 copy-start.2
  0.6 0.9 %copy.6.left = bf16[128,192]{1,0:T(8,128)(2,1)S(1)} copy(bf16[128,192]{0,1:T(8,128)(2,1)} %param.6) | data formatting | bytes 98304 | tf_op args[2]
  1.6 0.0 copy-done.2
  1.6 0.0 copy-start
  1.6 0.0 copy-start.1
  1.6 0.1 copy.7.right
  1.7 0.6 copy-done
  2.3 0.0 copy-done.1
  2.3 65.8 %shard_map.59 = (f32[64,192]{1,0:T(8,128)S(1)}, f32[64,192]{1,0:T(8,128)S(1)}) custom-call(bf16[64,192]{1,0:T(8,128)(2,1)S(1)} %copy-done, bf16[64,192]{1,0:T(8,128)(2,1)S(1)} %copy-done.1, bf16[128,192]{1,0:T(8,128)(2,1)S(1)} %copy.6.left, bf16[128,192]{1,0:T(8,128)(2,1)S(1)} %copy.7.right), custom_call_target="tpu_custom_call" | custom-call | flops 7247757312 | bytes 262144 | tf_op jit(solution)/shard_map/pallas_call | solution.py:187
  68.1 0.6 copy.10
  68.8 0.6 copy.11
Async XLA Ops:
  0.6 0.9 %copy-start.2 = (bf16[128,192]{0,1:T(8,128)(2,1)S(1)}, bf16[128,192]{0,1:T(8,128)(2,1)}, u32[]{:S(2)}) copy-start(bf16[128,192]{0,1:T(8,128)(2,1)} %param.7) | copy-start | bytes 147460
  1.6 0.8 %copy-start = (bf16[64,192]{1,0:T(8,128)(2,1)S(1)}, bf16[64,192]{1,0:T(8,128)(2,1)}, u32[]{:S(2)}) copy-start(bf16[64,192]{1,0:T(8,128)(2,1)} %source.1) | copy-start | bytes 73732
  1.6 0.8 %copy-start.1 = (bf16[64,192]{1,0:T(8,128)(2,1)S(1)}, bf16[64,192]{1,0:T(8,128)(2,1)}, u32[]{:S(2)}) copy-start(bf16[64,192]{1,0:T(8,128)(2,1)} %target.1) | copy-start | bytes 73732

commit v2 on v1

v2 whole, which is shorter than its diff:
```python
import functools

import jax
import jax.numpy as jnp
from jax import lax
from jax.experimental import pallas as pl
from jax.experimental.pallas import tpu as pltpu
from jax.sharding import PartitionSpec as P

MESH = pl.DeviceIdType.MESH
f32, bf16 = jnp.float32, jnp.bfloat16

E = 64
R = 128
B = 192
LANES = E + 64 + R
GROUP = 16
CHUNK = 4 * B
H = B // 2
ONE_X, ONE_Y = E + 3, E

RING = [0, 1, 3, 2]
LINE = [0, 1, 7, 2, 6, 3, 5, 4]

ORDER = [(0, 0), (0, 1), (2, 0), (2, 1), (0, 2), (2, 2), (1, 2), (1, 1), (0, 3), (2, 3), (1, 3), (3, 3), (3, 2), (3, 1), (3, 0), (1, 0)]
PASS_ON = {
    0: [(1, 0), (2, 0), (1, 1), (2, 1)],
    1: [(3, 0), (4, 0), (3, 1), (4, 1)],
    2: [(5, 0), (6, 1), (5, 1), (6, 0)],
    5: [(7, 0), (7, 1)],
}

NN = (((1,), (0,)), ((), ()))
NT = (((1,), (1,)), ((), ()))


def dot(a, b, dims):
    return lax.dot_general(a, b, dims, preferred_element_type=f32)


def prepare(embed_ref, factor_ref, first, rows_ref, places, stack):
    wide = embed_ref[...].astype(f32)
    half = -0.5 * jnp.sum(wide * wide, axis=0, keepdims=True)
    high = half.astype(bf16).astype(f32)
    middle = (half - high).astype(bf16).astype(f32)
    low = half - high - middle
    place = lax.broadcasted_iota(jnp.int32, (E, B), 0)
    norms, ones = (0, 3) if first else (3, 0)
    extra = jnp.where((place >= ones) & (place < ones + 3), 1.0, 0.0)
    for at, piece in enumerate((high, middle, low)):
        extra = jnp.where(place == norms + at, piece, extra)
    stack[0:E, :] = embed_ref[...]
    stack[E : 2 * E, :] = extra.astype(bf16)
    down = lax.broadcasted_iota(jnp.int32, (B, B), 0)
    along = lax.broadcasted_iota(jnp.int32, (B, B), 1)
    unit = jnp.where(down == along, 1.0, 0.0).astype(bf16)
    left_lanes = dot(unit, stack[...], NT).astype(bf16)
    for half, at in enumerate(places):
        rows_ref[at : at + H, 0 : 2 * E] = left_lanes[half * H : (half + 1) * H]
        rows_ref[at : at + H, 2 * E : LANES] = factor_ref[half * H : (half + 1) * H, :]


def pack(block):
    n = block.shape[0] // 2
    lane = lax.broadcasted_iota(jnp.int32, (n, 128), 1)
    return jnp.where(lane < E, block[0:n], pltpu.roll(block[n:], E, 1)).astype(bf16)


def unpack(total, runs, out_ref):
    tall = jnp.concatenate([total, jnp.zeros((128 - H, 128), f32)], axis=0).T
    size = B // len(runs)
    lane = lax.broadcasted_iota(jnp.int32, (E, 128), 1)
    for begin in (0, 128):
        piece = jnp.zeros((E, 128), f32)
        for at, row, half in runs:
            if at < begin + 128 and at + size > begin:
                moved = pltpu.roll(tall[half * E : (half + 1) * E, :], (at - begin - row) % 128, 1)
                inside = (lane >= at - begin) & (lane < at - begin + size)
                piece = jnp.where(inside, moved, piece)
        width = min(128, B - begin)
        out_ref[:, begin : begin + width] = piece[:, 0:width]


def kernel(source, target, left, right, out_s, out_t, xa, ya, xt, rp, cp, stack, own, send_r, recv_r, mine, theirs, given, send_c, recv_c, *sems):
    in_sems, gx_s, gx_r, gz_s, gz_r, gc_s, gc_r, rr_s, rr_r, rc_s, rc_r, rz_s, rz_r = sems
    row, col = lax.axis_index("row"), lax.axis_index("col")
    y, z, core = row // 2, col // 4, col % 2
    x = (col // 2) % 2 * 2 + row % 2
    own_embed, own_factor = own

    def device(x, y, z, core):
        return (y % 4 * 2 + x % 2, (z % 8 * 2 + x % 4 // 2) * 2 + core)

    def frames_of(h, k, i, sign):
        dx, dy = (RING[i], RING[k]) if h == 0 else (RING[k], RING[i])
        return device(x + sign * dx % 4, y + sign * dy % 4, z, core)

    line_owner = [device(x, y, z + 8 - dz, core) for dz in LINE]
    up, down, sibling = device(x, y, z + 1, core), device(x, y, z + 7, core), device(x, y, z, 1 - core)

    def copy(src, dst, send, recv, peer):
        return pltpu.make_async_remote_copy(
            src_ref=src, dst_ref=dst, send_sem=send, recv_sem=recv, device_id=peer, device_id_type=MESH
        )

    def place(h, k, i):
        return (8 * k + 4 * h + i) * H

    def first_step(h, i):
        sem = 4 * h + i
        peer = frames_of(h, 0, i, 1)
        return copy(xa.at[pl.ds(place(h, 0, 0), H), :], xa.at[pl.ds(place(h, 0, i), H), :], gx_s.at[sem], gx_r.at[sem], peer)

    def second_step(h, k):
        sem = 8 + 4 * h + k
        peer = frames_of(h, k, 0, 1)
        return copy(xa.at[pl.ds(place(h, 0, 0), 4 * H), :], xa.at[pl.ds(place(h, k, 0), 4 * H), :], gx_s.at[sem], gx_r.at[sem], peer)

    def hop(p, half):
        before = {1: 0, 2: 0, 3: 1, 4: 2, 5: 3, 6: 4, 7: 5 + half}[p]
        at, old = 2 * p * B + half * H, 2 * before * B + half * H
        peer = up if before % 2 and p > 2 or p == 1 else down
        return copy(ya.at[pl.ds(old, H), :], ya.at[pl.ds(at, H), :], gz_s.at[2 * p + half], gz_r.at[2 * p + half], peer)

    def share(p):
        return copy(ya.at[pl.ds(2 * p * B, B), :], ya.at[pl.ds((2 * p + 1) * B, B), :], gc_s.at[p], gc_r.at[p], sibling)

    def give_r(h, k, i):
        slot = 8 * k + 4 * h + i
        return copy(send_r.at[slot], recv_r.at[slot], rr_s.at[slot], rr_r.at[slot], frames_of(h, k, i, -1))

    def give_pair(p):
        return copy(given.at[p], theirs.at[p], rc_s.at[p], rc_r.at[p], sibling)

    def give_z(p):
        return copy(send_c.at[p], recv_c.at[p], rz_s.at[p], rz_r.at[p], line_owner[p])

    blocks = [(h, k, i) for k in range(4) for h in range(2) for i in range(4) if k or i]
    reads = [
        pltpu.make_async_copy(src, dst, in_sems.at[n])
        for n, (src, dst) in enumerate(zip((target, right, source, left), (own_embed.at[0], own_factor.at[0], own_embed.at[1], own_factor.at[1])))
    ]
    for read in reads:
        read.start()
    barrier = pltpu.get_barrier_semaphore()
    greet = [frames_of(0, k, i, 1) for h, k, i in blocks if h == 0] + line_owner[1:] + [sibling]
    for peer in greet:
        pl.semaphore_signal(barrier, inc=1, device_id=peer, device_id_type=MESH)
    for read in reads:
        read.wait()
    prepare(own_embed.at[0], own_factor.at[0], False, ya, (0, H), stack)
    prepare(own_embed.at[1], own_factor.at[1], True, xa, (place(0, 0, 0), place(1, 0, 0)), stack)
    pl.semaphore_wait(barrier, len(greet))
    for half in range(2):
        hop(1, half).start()
        hop(2, half).start()
    for i in range(1, 4):
        for h in range(2):
            first_step(h, i).start()
    share(0).start()
    rp[...] = jnp.zeros_like(rp)
    cp[...] = jnp.zeros_like(cp)

    def arrive_x(chunk):
        for h in range(2):
            if chunk == 0:
                for i in range(1, 4):
                    first_step(h, i).wait_recv()
                for k in range(1, 4):
                    second_step(h, k).start()
            else:
                second_step(h, chunk).wait_recv()
        rows = slice(chunk * CHUNK, (chunk + 1) * CHUNK)
        xt[:, rows] = xa[rows, 0:128].T

    def pass_on(p, half):
        hop(p, half).wait_recv()
        if p < 5:
            hop(p + 2, half).start()
        elif p == 5 + half:
            hop(7, half).start()
        if half == last_half[p]:
            share(p).start()

    last_half = {p: half for at in sorted(PASS_ON) for p, half in PASS_ON[at]}

    def arrive_y(chunk):
        for p in (2 * chunk, 2 * chunk + 1):
            share(p).wait_recv()

    def grads(pulls, mass, embeds):
        return pulls - pulls[:, mass : mass + 1] * embeds.astype(f32)

    def finish_rows(chunk):
        at = slice(chunk * CHUNK, (chunk + 1) * CHUNK)
        part = grads(rp[at, :], ONE_Y, xa[at, 0:128])
        for h in range(2):
            for i in range(4):
                n = 4 * h + i
                slot = 8 * chunk + n
                packed = pack(part[n * H : (n + 1) * H])
                if chunk == 0 and i == 0:
                    recv_r[slot] = packed
                else:
                    send_r[slot] = packed
                    give_r(h, chunk, i).start()

    def finish_cols(chunk):
        at = slice(chunk * CHUNK, (chunk + 1) * CHUNK)
        part = grads(cp[:, at].T, ONE_X, ya[at, 0:128])
        for i in range(2):
            p = 2 * chunk + i
            given[p] = pack(part[(2 * i + 1) * B : (2 * i + 2) * B])
            give_pair(p).start()
            mine[p] = pack(part[2 * i * B : (2 * i + 1) * B])

    def combine_cols(chunk):
        for p in (2 * chunk, 2 * chunk + 1):
            give_pair(p).wait_recv()
            both = (mine[p].astype(f32) + theirs[p].astype(f32)).astype(bf16)
            if p == 0:
                recv_c[0] = both
            else:
                send_c[p] = both
                give_z(p).start()

    firsts = {}
    for i, (r, c) in enumerate(ORDER):
        if i in PASS_ON:
            firsts.setdefault(i, []).extend(functools.partial(pass_on, p, half) for p, half in PASS_ON[i])
        if all(c != a for _, a in ORDER[:i]):
            firsts.setdefault(i, []).append(functools.partial(arrive_y, c))
        if all(r != a for a, _ in ORDER[:i]):
            firsts.setdefault(i, []).append(functools.partial(arrive_x, r))
    lasts = {}
    for i, (r, c) in enumerate(ORDER):
        if all(c != a for _, a in ORDER[i + 1 :]):
            lasts.setdefault(i, []).append(functools.partial(finish_cols, c))
            lasts.setdefault(min(i + 1, len(ORDER) - 1), []).append(functools.partial(combine_cols, c))
        if all(r != a for a, _ in ORDER[i + 1 :]):
            lasts.setdefault(i, []).append(functools.partial(finish_rows, r))

    last = len(ORDER) - 1
    lasts[last] = sorted(lasts[last], key=lambda f: f.func is combine_cols)

    def at_tile(t, table):
        for i, steps in table.items():

            @pl.when(t == i)
            def _():
                for step in steps:
                    step()

    def tile(t, _):
        rb = sum(jnp.where(t == i, r, 0) for i, (r, _) in enumerate(ORDER))
        cb = sum(jnp.where(t == i, c, 0) for i, (_, c) in enumerate(ORDER))
        at_tile(t, firsts)
        rows = pl.ds(pl.multiple_of(rb * CHUNK, CHUNK), CHUNK)
        cols = pl.ds(pl.multiple_of(cb * CHUNK, CHUNK), CHUNK)
        arg = dot(xa[rows, 0:128], ya[cols, 0:128], NT)
        adjoint = dot(xa[rows, 128:256], ya[cols, 128:256], NT)
        weighted = (adjoint * jnp.exp(arg)).astype(bf16)
        rp[rows, :] += dot(weighted, ya[cols, 0:128], NN)
        cp[0:80, cols] += dot(xt[0:80, rows], weighted, NN)
        at_tile(t, lasts)
        return 0

    lax.fori_loop(0, len(ORDER), tile, 0)

    for h, k, i in blocks:
        give_r(h, k, i).wait_recv()
    halves = []
    for h in range(2):
        slots = [8 * k + 4 * h + i for k in range(4) for i in range(4)]
        halves.append(sum(recv_r[slot].astype(f32) for slot in slots))
    quarter = H // 2
    unpack(jnp.concatenate(halves, axis=0), [(0, 0, 0), (quarter, 0, 1), (H, quarter, 0), (H + quarter, quarter, 1)], out_s)
    for p in range(1, GROUP // 2):
        give_z(p).wait_recv()
    unpack(sum(recv_c[p].astype(f32) for p in range(GROUP // 2)), [(0, 0, 0), (H, 0, 1)], out_t)
    for h, k, i in blocks:
        give_r(h, k, i).wait_send()
        if k == 0:
            first_step(h, i).wait_send()
        elif i == 0:
            second_step(h, k).wait_send()
    for p in range(GROUP // 2):
        share(p).wait_send()
        give_pair(p).wait_send()
        if p > 0:
            give_z(p).wait_send()
            hop(p, 0).wait_send()
            hop(p, 1).wait_send()


def per_device(source_embed, target_embed, left_factor, right_factor):
    frames = GROUP * B
    vmem = pl.BlockSpec(memory_space=pltpu.VMEM)
    return pl.pallas_call(
        kernel,
        out_shape=(jax.ShapeDtypeStruct((E, B), f32),) * 2,
        in_specs=[pl.BlockSpec(memory_space=pl.ANY)] * 4,
        out_specs=(vmem,) * 2,
        scratch_shapes=[
            pltpu.VMEM((frames, LANES), bf16),
            pltpu.VMEM((frames, LANES), bf16),
            pltpu.VMEM((128, frames), bf16),
            pltpu.VMEM((frames, 128), f32),
            pltpu.VMEM((128, frames), f32),
            pltpu.VMEM((2 * E, B), bf16),
            [pltpu.VMEM((2, E, B), bf16), pltpu.VMEM((2, B, R), bf16)],
        ]
        + [pltpu.VMEM((2 * GROUP, H // 2, 128), bf16)] * 2
        + [pltpu.VMEM((GROUP // 2, H, 128), bf16)] * 5
        + [pltpu.SemaphoreType.DMA((4,))]
        + [pltpu.SemaphoreType.DMA((GROUP,))] * 6
        + [pltpu.SemaphoreType.DMA((2 * GROUP,))] * 2
        + [pltpu.SemaphoreType.DMA((GROUP,))] * 4,
        compiler_params=pltpu.CompilerParams(
            collective_id=0, has_side_effects=True, vmem_limit_bytes=60 << 20
        ),
        cost_estimate=pl.CostEstimate(
            flops=2 * frames * frames * (2 * E + 2 * E + R), bytes_accessed=1 << 18, transcendentals=frames * frames
        ),
    )(source_embed, target_embed, left_factor.T, right_factor.T)


def solution(mesh):
    spec = P(None, ("row", "col"))
    return jax.shard_map(
        per_device, mesh=mesh, in_specs=(spec,) * 4, out_specs=(spec,) * 2, check_vma=False
    )
```

time: 69.6 us -> 55.4 us (0.80)
  the two profiles are of different devices: /device:TPU:37 before, /device:TPU:1 now
where the time goes in v2:
time: 55.4 us; the launch traced here: 55.3 us
  Pallas kernels  52.5 us (95%)
  local copies, waits for them, and re-layouts  2.14 us (4%)
  between operations  0.65 us (1%)
    pallas_call x1, Pallas kernels, per_device(): pl.pallas_call(kernel, out_shape=(jax.ShapeDtypeStruct((E, B), f32),) * 2...  52.5 us
    unnamed x4, local copies, waits for them, and re-layouts  2.14 us

profile of v2, /device:TPU:1, one launch (start us, length us, event | category | flops | bytes accessed | tf_op | source)
XLA Modules:
  0.0 55.3 jit_solution(16042918565030183035)
XLA Ops:
  0.6 52.5 %shard_map.59 = (f32[64,192]{1,0:T(8,128)}, f32[64,192]{1,0:T(8,128)}) custom-call(bf16[64,192]{1,0:T(8,128)(2,1)} %source.1, bf16[64,192]{1,0:T(8,128)(2,1)} %target.1, bf16[192,128]{1,0:T(8,128)(2,1)} %bitcast.2, bf16[192,128]{1,0:T(8,128)(2,1)} %bitcast.3), custom_call_target="tpu_custom_call" | custom-call | flops 7247757312 | bytes 262144 | tf_op jit(solution)/shard_map/pallas_call | solution.py:299
  53.1 0.0 copy-start
  53.1 1.5 %copy.8 = f32[64,192]{1,0:T(8,128)} copy(f32[64,192]{1,0:T(8,128)} %get-tuple-element.4) | data formatting | bytes 98304
  54.6 0.0 copy-done
  54.6 0.6 %copy.9 = f32[64,192]{1,0:T(8,128)} copy(f32[64,192]{1,0:T(8,128)S(1)} %copy-done) | data formatting | bytes 98304
Async XLA Ops:
  53.1 1.5 %copy-start = (f32[64,192]{1,0:T(8,128)S(1)}, f32[64,192]{1,0:T(8,128)}, u32[]{:S(2)}) copy-start(f32[64,192]{1,0:T(8,128)} %get-tuple-element.5) | copy-start | bytes 147460

commit v3 on v2

v3 whole, which is shorter than its diff:
```python
import functools

import jax
import jax.numpy as jnp
from jax import lax
from jax.experimental import pallas as pl
from jax.experimental.pallas import tpu as pltpu
from jax.sharding import PartitionSpec as P

MESH = pl.DeviceIdType.MESH
f32, bf16 = jnp.float32, jnp.bfloat16

E = 64
R = 128
B = 192
LANES = E + 64 + R
GROUP = 16
H = B // 2
ONE_X, ONE_Y = E + 3, E

RING = [0, 1, 3, 2]
SLOTS = [(h, 0, i) for h in range(2) for i in range(4)] + [(h, k, 0) for h in range(2) for k in (1, 2)]
SLOTS += [(h, k, i) for h in range(2) for k in (1, 2) for i in (1, 2, 3)] + [(h, 3, i) for h in range(2) for i in range(4)]
LINE = [0, 1, 7, 2, 6, 3, 5, 4]

ROWS = [(0, 1024), (1024, 2304), (2304, 3072)]
COLS = [(0, 1024), (1024, 1792), (1792, 3072)]
TILES = [(0, 0), (0, 1), (1, 0), (1, 1), (0, 2), (1, 2), (2, 2), (2, 1), (2, 0)]

NN = (((1,), (0,)), ((), ()))
NT = (((1,), (1,)), ((), ()))


def dot(a, b, dims):
    return lax.dot_general(a, b, dims, preferred_element_type=f32)


def prepare(embed_ref, factor_ref, first, rows_ref, places, stack):
    wide = embed_ref[...].astype(f32)
    half = -0.5 * jnp.sum(wide * wide, axis=0, keepdims=True)
    high = half.astype(bf16).astype(f32)
    middle = (half - high).astype(bf16).astype(f32)
    low = half - high - middle
    place = lax.broadcasted_iota(jnp.int32, (E, B), 0)
    norms, ones = (0, 3) if first else (3, 0)
    extra = jnp.where((place >= ones) & (place < ones + 3), 1.0, 0.0)
    for at, piece in enumerate((high, middle, low)):
        extra = jnp.where(place == norms + at, piece, extra)
    stack[0:E, :] = embed_ref[...]
    stack[E : 2 * E, :] = extra.astype(bf16)
    down = lax.broadcasted_iota(jnp.int32, (B, B), 0)
    along = lax.broadcasted_iota(jnp.int32, (B, B), 1)
    unit = jnp.where(down == along, 1.0, 0.0).astype(bf16)
    left_lanes = dot(unit, stack[...], NT).astype(bf16)
    for half, at in enumerate(places):
        rows_ref[at : at + H, 0 : 2 * E] = left_lanes[half * H : (half + 1) * H]
        rows_ref[at : at + H, 2 * E : LANES] = factor_ref[half * H : (half + 1) * H, :]


def pack(block):
    n = block.shape[0] // 2
    lane = lax.broadcasted_iota(jnp.int32, (n, 128), 1)
    return jnp.where(lane < E, block[0:n], pltpu.roll(block[n:], E, 1)).astype(bf16)


def unpack(total, runs, out_ref):
    tall = jnp.concatenate([total, jnp.zeros((128 - H, 128), f32)], axis=0).T
    size = B // len(runs)
    lane = lax.broadcasted_iota(jnp.int32, (E, 128), 1)
    for begin in (0, 128):
        piece = jnp.zeros((E, 128), f32)
        for at, row, half in runs:
            if at < begin + 128 and at + size > begin:
                moved = pltpu.roll(tall[half * E : (half + 1) * E, :], (at - begin - row) % 128, 1)
                inside = (lane >= at - begin) & (lane < at - begin + size)
                piece = jnp.where(inside, moved, piece)
        width = min(128, B - begin)
        out_ref[:, begin : begin + width] = piece[:, 0:width]


def kernel(source, target, left, right, out_s, out_t, xa, ya, xt, rp, cp, stack, own, send_r, recv_r, mine, theirs, given, send_c, recv_c, *sems):
    in_sems, gx_s, gx_r, gz_s, gz_r, gc_s, gc_r, rr_s, rr_r, rc_s, rc_r, rz_s, rz_r = sems
    row, col = lax.axis_index("row"), lax.axis_index("col")
    y, z, core = row // 2, col // 4, col % 2
    x = (col // 2) % 2 * 2 + row % 2
    own_embed, own_factor = own

    def device(x, y, z, core):
        return (y % 4 * 2 + x % 2, (z % 8 * 2 + x % 4 // 2) * 2 + core)

    def frames_of(h, k, i, sign):
        dx, dy = (RING[i], RING[k]) if h == 0 else (RING[k], RING[i])
        return device(x + sign * dx % 4, y + sign * dy % 4, z, core)

    line_owner = [device(x, y, z + 8 - dz, core) for dz in LINE]
    line_to = [device(x, y, z + dz, core) for dz in LINE]
    sibling = device(x, y, z, 1 - core)

    def copy(src, dst, send, recv, peer):
        return pltpu.make_async_remote_copy(
            src_ref=src, dst_ref=dst, send_sem=send, recv_sem=recv, device_id=peer, device_id_type=MESH
        )

    def place(h, k, i):
        return SLOTS.index((h, k, i)) * H

    def step_x(h, k, i, n=1):
        old = place(h, 0, i) if k else place(h, 0, 0)
        at = SLOTS.index((h, k, i))
        peer = frames_of(h, k, 0, 1) if k else frames_of(h, 0, i, 1)
        return copy(xa.at[pl.ds(old, n * H), :], xa.at[pl.ds(at * H, n * H), :], gx_s.at[at], gx_r.at[at], peer)

    def hop(p, half=None):
        if p < 5:
            old, at, size, peer = 0, 2 * p * B, B, line_to[p]
        elif p < 7:
            old, at, size, peer = 2 * (p - 2) * B, 2 * p * B, B, line_to[p - 4]
        else:
            off = half * H
            old, at, size, peer = 2 * (3 + half) * B + off, 2 * p * B + off, H, line_to[3 + half]
        sem = p + (half or 0)
        return copy(ya.at[pl.ds(old, size), :], ya.at[pl.ds(at, size), :], gz_s.at[sem], gz_r.at[sem], peer)

    def share(p):
        return copy(ya.at[pl.ds(2 * p * B, B), :], ya.at[pl.ds((2 * p + 1) * B, B), :], gc_s.at[p], gc_r.at[p], sibling)

    def give_r(h, k, i):
        slot = SLOTS.index((h, k, i))
        return copy(send_r.at[slot], recv_r.at[slot], rr_s.at[slot], rr_r.at[slot], frames_of(h, k, i, -1))

    def give_pair(p):
        return copy(given.at[p], theirs.at[p], rc_s.at[p], rc_r.at[p], sibling)

    def give_z(p):
        return copy(send_c.at[p], recv_c.at[p], rz_s.at[p], rz_r.at[p], line_owner[p])

    blocks = [block for block in SLOTS if block[1] or block[2]]
    near = [(h, 0, i) for i in range(1, 4) for h in range(2)] + [(h, k, 0) for h in range(2) for k in (1, 2)]
    later = [(h, k, 1, 3) for k in (1, 2) for h in range(2)]
    far = [(h, 3, 0, 4) for h in range(2)]
    reads = [
        pltpu.make_async_copy(src, dst, in_sems.at[n])
        for n, (src, dst) in enumerate(zip((target, right, source, left), (own_embed.at[0], own_factor.at[0], own_embed.at[1], own_factor.at[1])))
    ]
    for read in reads:
        read.start()
    barrier = pltpu.get_barrier_semaphore()
    greet = [frames_of(0, k, i, 1) for h, k, i in blocks if h == 0] + line_owner[1:] + [sibling]
    for peer in greet:
        pl.semaphore_signal(barrier, inc=1, device_id=peer, device_id_type=MESH)
    for read in reads:
        read.wait()
    prepare(own_embed.at[0], own_factor.at[0], False, ya, (0, H), stack)
    prepare(own_embed.at[1], own_factor.at[1], True, xa, (place(0, 0, 0), place(1, 0, 0)), stack)
    pl.semaphore_wait(barrier, len(greet))
    for p in (1, 2):
        hop(p).start()
    for block in near:
        step_x(*block).start()
    for p in (3, 4):
        hop(p).start()
    share(0).start()
    cp[80:128, :] = jnp.zeros((48, cp.shape[1]), f32)

    def arrive_x(blocks, begin, end):
        for block in blocks:
            step_x(*block).wait_recv()
        xt[:, begin:end] = xa[begin:end, 0:128].T

    def send_later():
        for steps in later:
            step_x(*steps).start()

    def send_far():
        for steps in far:
            step_x(*steps).start()

    def arrive_z(p):
        if p < 7:
            hop(p).wait_recv()
        else:
            hop(7, 0).wait_recv()
            hop(7, 1).wait_recv()
        if p in (3, 4):
            hop(p + 2).start()
            hop(7, p - 3).start()
        share(p).start()

    def arrive_y(*pairs):
        for p in pairs:
            share(p).wait_recv()

    def grads(pulls, mass, embeds):
        return pulls - pulls[:, mass : mass + 1] * embeds.astype(f32)

    def finish_rows(begin, end):
        at = slice(begin * H, end * H)
        part = grads(rp[at, :], ONE_Y, xa[at, 0:128])
        for slot in range(begin, end):
            packed = pack(part[(slot - begin) * H : (slot - begin + 1) * H])
            if SLOTS[slot] in blocks:
                send_r[slot] = packed
                give_r(*SLOTS[slot]).start()
            else:
                recv_r[slot] = packed

    def finish_cols(*pairs):
        begin, end = 2 * pairs[0] * B, 2 * (pairs[-1] + 1) * B
        part = grads(cp[:, begin:end].T, ONE_X, ya[begin:end, 0:128])
        for i, p in enumerate(pairs):
            given[p] = pack(part[(2 * i + 1) * B : (2 * i + 2) * B])
            give_pair(p).start()
            mine[p] = pack(part[2 * i * B : (2 * i + 1) * B])

    def combine_cols(*pairs):
        for p in pairs:
            give_pair(p).wait_recv()
            both = (mine[p].astype(f32) + theirs[p].astype(f32)).astype(bf16)
            if p == 0:
                recv_c[0] = both
            else:
                send_c[p] = both
                give_z(p).start()

    def tile(r, c):
        rows, cols = slice(*ROWS[r]), slice(*COLS[c])
        arg = dot(xa[rows, 0:128], ya[cols, 0:128], NT)
        adjoint = dot(xa[rows, 128:256], ya[cols, 128:256], NT)
        weighted = (adjoint * jnp.exp(arg)).astype(bf16)
        pulls = dot(weighted, ya[cols, 0:128], NN)
        rp[rows, :] = pulls if TILES.index((r, c)) == min(TILES.index((r, b)) for b in range(3)) else rp[rows, :] + pulls
        pulls = dot(xt[0:80, rows], weighted, NN)
        cp[0:80, cols] = pulls if r == 0 else cp[0:80, cols] + pulls

    arrive_z(1)
    arrive_z(2)
    arrive_x(near, 0, 12 * H)
    send_later()
    arrive_y(0, 1, 2)
    tile(0, 0)
    arrive_z(3)
    arrive_z(4)
    send_far()
    arrive_y(3, 4)
    tile(0, 1)
    arrive_x(later, 12 * H, 24 * H)
    tile(1, 0)
    arrive_z(5)
    arrive_z(6)
    tile(1, 1)
    arrive_z(7)
    arrive_y(5, 6, 7)
    tile(0, 2)
    finish_rows(0, 10)
    tile(1, 2)
    finish_rows(10, 24)
    arrive_x(far, 24 * H, 32 * H)
    tile(2, 2)
    finish_cols(5, 6, 7)
    tile(2, 1)
    finish_cols(3, 4)
    combine_cols(5, 6, 7)
    tile(2, 0)
    finish_cols(0, 1, 2)
    finish_rows(24, 32)
    combine_cols(3, 4)
    combine_cols(0, 1, 2)

    for h, k, i in blocks:
        give_r(h, k, i).wait_recv()
    halves = []
    for h in range(2):
        slots = [slot for slot, block in enumerate(SLOTS) if block[0] == h]
        halves.append(sum(recv_r[slot].astype(f32) for slot in slots))
    quarter = H // 2
    unpack(jnp.concatenate(halves, axis=0), [(0, 0, 0), (quarter, 0, 1), (H, quarter, 0), (H + quarter, quarter, 1)], out_s)
    for p in range(1, GROUP // 2):
        give_z(p).wait_recv()
    unpack(sum(recv_c[p].astype(f32) for p in range(GROUP // 2)), [(0, 0, 0), (H, 0, 1)], out_t)
    for h, k, i in blocks:
        give_r(h, k, i).wait_send()
    for p in range(GROUP // 2):
        share(p).wait_send()
        give_pair(p).wait_send()
        if p > 0:
            give_z(p).wait_send()
        if 0 < p < 7:
            hop(p).wait_send()
    for half in range(2):
        hop(7, half).wait_send()
    for steps in near + later + far:
        step_x(*steps).wait_send()


def per_device(source_embed, target_embed, left_factor, right_factor):
    frames = GROUP * B
    vmem = pl.BlockSpec(memory_space=pltpu.VMEM)
    return pl.pallas_call(
        kernel,
        out_shape=(jax.ShapeDtypeStruct((E, B), f32),) * 2,
        in_specs=[pl.BlockSpec(memory_space=pltpu.HBM)] * 4,
        out_specs=(vmem,) * 2,
        scratch_shapes=[
            pltpu.VMEM((frames, LANES), bf16),
            pltpu.VMEM((frames, LANES), bf16),
            pltpu.VMEM((128, frames), bf16),
            pltpu.VMEM((frames, 128), f32),
            pltpu.VMEM((128, frames), f32),
            pltpu.VMEM((2 * E, B), bf16),
            [pltpu.VMEM((2, E, B), bf16), pltpu.VMEM((2, B, R), bf16)],
        ]
        + [pltpu.VMEM((2 * GROUP, H // 2, 128), bf16)] * 2
        + [pltpu.VMEM((GROUP // 2, H, 128), bf16)] * 5
        + [pltpu.SemaphoreType.DMA((4,))]
        + [pltpu.SemaphoreType.DMA((2 * GROUP,))] * 2
        + [pltpu.SemaphoreType.DMA((GROUP,))] * 4
        + [pltpu.SemaphoreType.DMA((2 * GROUP,))] * 2
        + [pltpu.SemaphoreType.DMA((GROUP,))] * 4,
        compiler_params=pltpu.CompilerParams(
            collective_id=0, has_side_effects=True, vmem_limit_bytes=56 << 20
        ),
        cost_estimate=pl.CostEstimate(
            flops=2 * frames * frames * (2 * E + 2 * E + R), bytes_accessed=1 << 18, transcendentals=frames * frames
        ),
    )(source_embed, target_embed, left_factor.T, right_factor.T)


def solution(mesh):
    spec = P(None, ("row", "col"))
    return jax.shard_map(
        per_device, mesh=mesh, in_specs=(spec,) * 4, out_specs=(spec,) * 2, check_vma=False
    )
```

time: 55.4 us -> 53.1 us (0.958)
  Pallas kernels: 52.5 us -> 50.1 us
    pallas_call x1, Pallas kernels: 52.5 us -> 50.1 us  [per_device(): pl.pallas_call(kernel, out_shape=(jax.ShapeDtypeStruct((E, B), f32),) * 2...]
where the time goes in v3:
time: 53.1 us; the launch traced here: 52.9 us
  Pallas kernels  50.1 us (94%)
  local copies, waits for them, and re-layouts  2.14 us (4%)
  between operations  0.65 us (1%)
    pallas_call x1, Pallas kernels, per_device(): pl.pallas_call(kernel, out_shape=(jax.ShapeDtypeStruct((E, B), f32),) * 2...  50.1 us
    unnamed x4, local copies, waits for them, and re-layouts  2.14 us

profile of v3, /device:TPU:1, one launch (start us, length us, event | category | flops | bytes accessed | tf_op | source)
XLA Modules:
  0.0 52.9 jit_solution(8604470496570324000)
XLA Ops:
  0.6 50.1 %shard_map.59 = (f32[64,192]{1,0:T(8,128)}, f32[64,192]{1,0:T(8,128)}) custom-call(bf16[64,192]{1,0:T(8,128)(2,1)} %source.1, bf16[64,192]{1,0:T(8,128)(2,1)} %target.1, bf16[192,128]{1,0:T(8,128)(2,1)} %bitcast.2, bf16[192,128]{1,0:T(8,128)(2,1)} %bitcast.3), custom_call_target="tpu_custom_call" | custom-call | flops 7247757312 | bytes 262144 | tf_op jit(solution)/shard_map/pallas_call | solution.py:298
  50.7 0.0 copy-start
  50.7 1.5 %copy.8 = f32[64,192]{1,0:T(8,128)} copy(f32[64,192]{1,0:T(8,128)} %get-tuple-element.4) | data formatting | bytes 98304
  52.2 0.0 copy-done
  52.2 0.6 %copy.9 = f32[64,192]{1,0:T(8,128)} copy(f32[64,192]{1,0:T(8,128)S(1)} %copy-done) | data formatting | bytes 98304
Async XLA Ops:
  50.7 1.5 %copy-start = (f32[64,192]{1,0:T(8,128)S(1)}, f32[64,192]{1,0:T(8,128)}, u32[]{:S(2)}) copy-start(f32[64,192]{1,0:T(8,128)} %get-tuple-element.5) | copy-start | bytes 147460

commit v4 on v3

--- a/solution.py
+++ b/solution.py
@@ -78,12 +78,13 @@
         out_ref[:, begin : begin + width] = piece[:, 0:width]
 
 
-def kernel(source, target, left, right, out_s, out_t, xa, ya, xt, rp, cp, stack, own, send_r, recv_r, mine, theirs, given, send_c, recv_c, *sems):
+def kernel(source, target, left, right, out, xa, ya, xt, rp, cp, stack, own, send_r, recv_r, mine, theirs, given, send_c, recv_c, *sems):
     in_sems, gx_s, gx_r, gz_s, gz_r, gc_s, gc_r, rr_s, rr_r, rc_s, rc_r, rz_s, rz_r = sems
     row, col = lax.axis_index("row"), lax.axis_index("col")
     y, z, core = row // 2, col // 4, col % 2
     x = (col // 2) % 2 * 2 + row % 2
     own_embed, own_factor = own
+    out_s, out_t = out.at[0], out.at[1]
 
     def device(x, y, z, core):
         return (y % 4 * 2 + x % 2, (z % 8 * 2 + x % 4 // 2) * 2 + core)
@@ -145,21 +146,23 @@
     for read in reads:
         read.start()
     barrier = pltpu.get_barrier_semaphore()
-    greet = [frames_of(0, k, i, 1) for h, k, i in blocks if h == 0] + line_owner[1:] + [sibling]
+    greet = [frames_of(h, 0, i, 1) for h in range(2) for i in range(1, 4)] + line_to[1:5] + [sibling]
     for peer in greet:
         pl.semaphore_signal(barrier, inc=1, device_id=peer, device_id_type=MESH)
-    for read in reads:
+    for read in reads[:2]:
         read.wait()
     prepare(own_embed.at[0], own_factor.at[0], False, ya, (0, H), stack)
+    for read in reads[2:]:
+        read.wait()
     prepare(own_embed.at[1], own_factor.at[1], True, xa, (place(0, 0, 0), place(1, 0, 0)), stack)
     pl.semaphore_wait(barrier, len(greet))
+    share(0).start()
     for p in (1, 2):
         hop(p).start()
     for block in near:
         step_x(*block).start()
     for p in (3, 4):
         hop(p).start()
-    share(0).start()
     cp[80:128, :] = jnp.zeros((48, cp.shape[1]), f32)
 
     def arrive_x(blocks, begin, end):
@@ -295,11 +298,11 @@
 def per_device(source_embed, target_embed, left_factor, right_factor):
     frames = GROUP * B
     vmem = pl.BlockSpec(memory_space=pltpu.VMEM)
-    return pl.pallas_call(
+    both = pl.pallas_call(
         kernel,
-        out_shape=(jax.ShapeDtypeStruct((E, B), f32),) * 2,
+        out_shape=jax.ShapeDtypeStruct((2, E, B), f32),
         in_specs=[pl.BlockSpec(memory_space=pltpu.HBM)] * 4,
-        out_specs=(vmem,) * 2,
+        out_specs=vmem,
         scratch_shapes=[
             pltpu.VMEM((frames, LANES), bf16),
             pltpu.VMEM((frames, LANES), bf16),
@@ -323,6 +326,7 @@
             flops=2 * frames * frames * (2 * E + 2 * E + R), bytes_accessed=1 << 18, transcendentals=frames * frames
         ),
     )(source_embed, target_embed, left_factor.T, right_factor.T)
+    return both[0], both[1]
 
 
 def solution(mesh):

time: 53.1 us -> 51.5 us (0.970)
  Pallas kernels: 50.1 us -> 49.1 us
  local copies, waits for them, and re-layouts: 2.14 us -> 1.53 us
    unnamed x4 -> x0, local copies, waits for them, and re-layouts: 2.14 us -> none
    squeeze x0 -> x1, local copies, waits for them, and re-layouts: none -> 1.53 us  [per_device(): return (both[0], both[1])]
    pallas_call x1, Pallas kernels: 50.1 us -> 49.1 us  [per_device(): pl.pallas_call(kernel, out_shape=jax.ShapeDtypeStruct((2, E, B), f32), in...]
where the time goes in v4:
time: 51.5 us; the launch traced here: 51.3 us
  Pallas kernels  49.1 us (95%)
  local copies, waits for them, and re-layouts  1.53 us (3%)
  between operations  0.64 us (1%)
    pallas_call x1, Pallas kernels, per_device(): pl.pallas_call(kernel, out_shape=jax.ShapeDtypeStruct((2, E, B), f32), in...  49.1 us
    squeeze x1, local copies, waits for them, and re-layouts, per_device(): return (both[0], both[1])  1.53 us

profile of v4, /device:TPU:1, one launch (start us, length us, event | category | flops | bytes accessed | tf_op | source)
XLA Modules:
  0.0 51.3 jit_solution(10283600168973691097)
XLA Ops:
  0.6 49.1 %shard_map.59 = f32[2,64,192]{2,1,0:T(8,128)} custom-call(bf16[64,192]{1,0:T(8,128)(2,1)} %source.1, bf16[64,192]{1,0:T(8,128)(2,1)} %target.1, bf16[192,128]{1,0:T(8,128)(2,1)} %bitcast.6, bf16[192,128]{1,0:T(8,128)(2,1)} %bitcast.7), custom_call_target="tpu_custom_call" | custom-call | flops 7247757312 | bytes 262144 | tf_op jit(solution)/shard_map/pallas_call | solution.py:301
  49.8 1.5 %slice_bitcast_fusion = (f32[64,192]{1,0:T(8,128)}, f32[64,192]{1,0:T(8,128)}) fusion(f32[2,64,192]{2,1,0:T(8,128)} %shard_map.59), kind=kLoop, calls=%fused_computation | loop fusion | bytes 196608 | tf_op jit(solution)/shard_map/squeeze | solution.py:329

commit v5 on v4

--- a/solution.py
+++ b/solution.py
@@ -264,9 +264,9 @@
     finish_cols(3, 4)
     combine_cols(5, 6, 7)
     tile(2, 0)
+    combine_cols(3, 4)
     finish_cols(0, 1, 2)
     finish_rows(24, 32)
-    combine_cols(3, 4)
     combine_cols(0, 1, 2)
 
     for h, k, i in blocks:

time: 51.5 us -> 51.7 us (level)
  no operation moved by 1% of the time
where the time goes in v5:
time: 51.7 us; the launch traced here: 51.5 us
  Pallas kernels  49.4 us (96%)
  local copies, waits for them, and re-layouts  1.53 us (3%)
  between operations  0.64 us (1%)
    pallas_call x1, Pallas kernels, per_device(): pl.pallas_call(kernel, out_shape=jax.ShapeDtypeStruct((2, E, B), f32), in...  49.4 us
    squeeze x1, local copies, waits for them, and re-layouts, per_device(): return (both[0], both[1])  1.53 us

profile of v5, /device:TPU:1, one launch (start us, length us, event | category | flops | bytes accessed | tf_op | source)
XLA Modules:
  0.0 51.5 jit_solution(12342466952900914710)
XLA Ops:
  0.6 49.4 %shard_map.59 = f32[2,64,192]{2,1,0:T(8,128)} custom-call(bf16[64,192]{1,0:T(8,128)(2,1)} %source.1, bf16[64,192]{1,0:T(8,128)(2,1)} %target.1, bf16[192,128]{1,0:T(8,128)(2,1)} %bitcast.6, bf16[192,128]{1,0:T(8,128)(2,1)} %bitcast.7), custom_call_target="tpu_custom_call" | custom-call | flops 7247757312 | bytes 262144 | tf_op jit(solution)/shard_map/pallas_call | solution.py:301
  50.0 1.5 %slice_bitcast_fusion = (f32[64,192]{1,0:T(8,128)}, f32[64,192]{1,0:T(8,128)}) fusion(f32[2,64,192]{2,1,0:T(8,128)} %shard_map.59), kind=kLoop, calls=%fused_computation | loop fusion | bytes 196608 | tf_op jit(solution)/shard_map/squeeze | solution.py:329
